TPU v7x, 32 devices: a whole 2x2x4 slice. The times are simulated.
32 devices in a mesh: img: 8 (over z, y), row: 4 (over x, core).
Axes of the slice: x: 2, y: 2, z: 4, core: 2. Of those that a mesh axis runs over, the one named last changes fastest.
Arguments:
- activations: bfloat16 [24, 16, 192, 512], P('img', 'row'), may hold values from -4 to 4
- cotangent: bfloat16 [24, 16, 192, 512], P('img', 'row'), may hold values from -6 to 6
- weights: bfloat16 [3147776], P(('img', 'row')), may hold values from -2 to 2
Outputs:
- block_out: bfloat16 [24, 16, 192, 512], P('img', 'row')
- input_grad: float32 [24, 16, 192, 512], P('img', 'row')
- weight_grad: float32 [3147776], P(('img', 'row'))
- summary_mean: float32 [512], replicated
- summary_var: float32 [512], replicated
All inputs are finite; a program needn't handle non-finite values.
Results may differ from a plain program's by a relative error of at most 0.0102.
Values may be sent and summed in bfloat16 or wider, within the bound.
No kernel may reach another device: no remote copies, remote signals or barrier semaphores. Data moves between devices by JAX's collectives and lax.ppermute only.
A program may use at most 256 MiB of HBM per device.

v0:
```python
import math

import jax
import jax.numpy as jnp
from jax import lax
from jax.sharding import PartitionSpec as P

FF = 2048
HEADS = 8


EPS = 1e-05
NEGATIVE = -1e30
HALF = jnp.bfloat16
SINGLE = jnp.float32


def unpack(flat_weights, model_width, ff_width):
    lengths = (
        [model_width] * 4
        + [model_width * model_width] * 4
        + [model_width * ff_width, ff_width * model_width]
    )
    segments = []
    offset = 0
    for length in lengths:
        segments.append(flat_weights[offset : offset + length])
        offset = offset + length
    layouts = [(model_width, model_width)] * 4 + [(model_width, ff_width), (ff_width, model_width)]
    matrices = [segment.reshape(layout) for segment, layout in zip(segments[4:], layouts)]
    vectors = [segment.astype(SINGLE) for segment in segments[:4]]
    return (vectors, matrices)


def normalize(values):
    centred = values - jnp.mean(values, axis=-1, keepdims=True)
    inverse = lax.rsqrt(jnp.mean(centred * centred, axis=-1, keepdims=True) + EPS)
    return (centred * inverse, inverse)


def norm_back(grad_norm, normed, inverse):
    return inverse * (
        grad_norm
        - jnp.mean(grad_norm, axis=-1, keepdims=True)
        - normed * jnp.mean(grad_norm * normed, axis=-1, keepdims=True)
    )


def forward_dot(left, right):
    return jnp.einsum("rwd,de->rwe", left, right, preferred_element_type=SINGLE)


def backward_dot(left, right):
    return jnp.einsum("rwe,de->rwd", left, right, preferred_element_type=SINGLE)


def outer_dot(left, right):
    return jnp.einsum("rwd,rwe->de", left, right, preferred_element_type=SINGLE)


def attention_probs(query_four, key_four, key_heads, row_mask, far_mask, scaling):
    own_scores = (
        jnp.einsum("rqhd,rkhd->rhqk", query_four, key_four, preferred_element_type=SINGLE) * scaling
    )
    far_scores = (
        jnp.einsum("rqhd,shd->rhqs", query_four, key_heads, preferred_element_type=SINGLE) * scaling
    )
    own_scores = jnp.where(row_mask[None, None], own_scores, NEGATIVE)
    far_scores = jnp.where(far_mask[:, None, None, :], far_scores, NEGATIVE)
    top_score = jnp.maximum(
        jnp.max(own_scores, axis=-1, keepdims=True), jnp.max(far_scores, axis=-1, keepdims=True)
    )
    own_exp = jnp.exp(own_scores - top_score)
    far_exp = jnp.exp(far_scores - top_score)
    exp_total = jnp.sum(own_exp, axis=-1, keepdims=True) + jnp.sum(far_exp, axis=-1, keepdims=True)
    return (own_exp / exp_total, far_exp / exp_total)


def per_device(activations, cotangent, weights):
    images, local_rows, columns, model_width = activations.shape
    head_width = model_width // HEADS
    scaling = 1.0 / math.sqrt(head_width)
    total_rows = local_rows * lax.axis_size("row")
    first_row = lax.axis_index("row") * local_rows
    summary_count = float(images * lax.axis_size("img") * total_rows)
    gathered = lax.all_gather(weights, ("img", "row"), axis=0, tiled=True)
    vectors, matrices = unpack(gathered, model_width, FF)
    gain_one, gain_sum, bias_sum, gain_two = vectors
    w_query, w_key, w_value, w_out, w_inner, w_outer = matrices
    row_means = jnp.mean(activations.astype(SINGLE), axis=2)
    local_first = jnp.sum(row_means, axis=(0, 1))
    local_second = jnp.sum(row_means * row_means, axis=(0, 1))
    total_first, total_second = lax.psum((local_first, local_second), ("img", "row"))
    summary_mean = total_first / summary_count
    summary_var = total_second / summary_count - summary_mean * summary_mean
    summary_inv = lax.rsqrt(summary_var + EPS)
    standard = (row_means - summary_mean) * summary_inv
    summary_low = (standard * gain_sum + bias_sum).astype(HALF)
    key_local = forward_dot(summary_low, w_key).astype(HALF)
    value_local = forward_dot(summary_low, w_value).astype(HALF)
    key_all, value_all = (
        lax.all_gather(key_local, "row", axis=1, tiled=True),
        lax.all_gather(value_local, "row", axis=1, tiled=True),
    )
    position = lax.broadcasted_iota(jnp.int32, (columns, columns), 0)
    key_position = lax.broadcasted_iota(jnp.int32, (columns, columns), 1)
    row_mask = key_position <= position
    global_rows = first_row + jnp.arange(local_rows, dtype=jnp.int32)
    far_mask = jnp.arange(total_rows, dtype=jnp.int32)[None, :] < global_rows[:, None]
    kept_values = []
    outputs = []
    for image_index in range(images):
        block_in = activations[image_index].astype(SINGLE)
        normed_one, inverse_one = normalize(block_in)
        attn_in = (normed_one * gain_one).astype(HALF)
        four_shape = (local_rows, columns, HEADS, head_width)
        query_four = forward_dot(attn_in, w_query).astype(HALF).reshape(four_shape)
        key_four = forward_dot(attn_in, w_key).astype(HALF).reshape(four_shape)
        value_four = forward_dot(attn_in, w_value).astype(HALF).reshape(four_shape)
        key_heads = key_all[image_index].reshape(total_rows, HEADS, head_width)
        value_heads = value_all[image_index].reshape(total_rows, HEADS, head_width)
        own_prob, far_prob = attention_probs(
            query_four, key_four, key_heads, row_mask, far_mask, scaling
        )
        own_low = own_prob.astype(HALF)
        far_low = far_prob.astype(HALF)
        mixed_heads = jnp.einsum(
            "rhqk,rkhd->rqhd", own_low, value_four, preferred_element_type=SINGLE
        )
        mixed_heads = mixed_heads + jnp.einsum(
            "rhqs,shd->rqhd", far_low, value_heads, preferred_element_type=SINGLE
        )
        mixed_low = mixed_heads.reshape(local_rows, columns, model_width).astype(HALF)
        middle = block_in + forward_dot(mixed_low, w_out)
        normed_two, inverse_two = normalize(middle)
        ff_in = (normed_two * gain_two).astype(HALF)
        inner_pre = forward_dot(ff_in, w_inner)
        activated = jax.nn.gelu(inner_pre).astype(HALF)
        outputs.append((middle + forward_dot(activated, w_outer)).astype(HALF))
        kept_values.append(
            (
                normed_one,
                inverse_one,
                attn_in,
                query_four,
                key_four,
                value_four,
                own_prob,
                far_prob,
                mixed_low,
                normed_two,
                inverse_two,
                ff_in,
                inner_pre,
                activated,
            )
        )
    regathered = lax.all_gather(weights, ("img", "row"), axis=0, tiled=True)
    vectors, matrices = unpack(regathered, model_width, FF)
    gain_one, gain_sum, bias_sum, gain_two = vectors
    w_query, w_key, w_value, w_out, w_inner, w_outer = matrices
    grad_gain_one = jnp.zeros((model_width,), SINGLE)
    grad_gain_two = jnp.zeros((model_width,), SINGLE)
    grad_query_w = jnp.zeros((model_width, model_width), SINGLE)
    grad_key_w = jnp.zeros((model_width, model_width), SINGLE)
    grad_value_w = jnp.zeros((model_width, model_width), SINGLE)
    grad_out_w = jnp.zeros((model_width, model_width), SINGLE)
    grad_inner_w = jnp.zeros((model_width, FF), SINGLE)
    grad_outer_w = jnp.zeros((FF, model_width), SINGLE)
    key_far_grads = []
    value_far_grads = []
    partial_inputs = []
    for image_index in range(images):
        (
            normed_one,
            inverse_one,
            attn_in,
            query_four,
            key_four,
            value_four,
            own_prob,
            far_prob,
            mixed_low,
            normed_two,
            inverse_two,
            ff_in,
            inner_pre,
            activated,
        ) = kept_values[image_index]
        key_heads = key_all[image_index].reshape(total_rows, HEADS, head_width)
        value_heads = value_all[image_index].reshape(total_rows, HEADS, head_width)
        out_grad = cotangent[image_index]
        grad_outer_w = grad_outer_w + outer_dot(activated, out_grad)
        act_grad = backward_dot(out_grad, w_outer)
        gelu_value, gelu_back = jax.vjp(jax.nn.gelu, inner_pre)
        inner_grad = gelu_back(act_grad)[0].astype(HALF)
        grad_inner_w = grad_inner_w + outer_dot(ff_in, inner_grad)
        ff_grad = backward_dot(inner_grad, w_inner)
        grad_gain_two = grad_gain_two + jnp.sum(ff_grad * normed_two, axis=(0, 1))
        middle_grad = out_grad.astype(SINGLE) + norm_back(
            ff_grad * gain_two, normed_two, inverse_two
        )
        branch_grad = middle_grad.astype(HALF)
        grad_out_w = grad_out_w + outer_dot(mixed_low, branch_grad)
        mixed_grad = (
            backward_dot(branch_grad, w_out)
            .astype(HALF)
            .reshape(local_rows, columns, HEADS, head_width)
        )
        own_dp = jnp.einsum(
            "rqhd,rkhd->rhqk", mixed_grad, value_four, preferred_element_type=SINGLE
        )
        far_dp = jnp.einsum(
            "rqhd,shd->rhqs", mixed_grad, value_heads, preferred_element_type=SINGLE
        )
        inner_sum = jnp.sum(own_dp * own_prob, axis=-1, keepdims=True) + jnp.sum(
            far_dp * far_prob, axis=-1, keepdims=True
        )
        own_dz = (own_prob * (own_dp - inner_sum)).astype(HALF)
        far_dz = (far_prob * (far_dp - inner_sum)).astype(HALF)
        query_grad = (
            jnp.einsum("rhqk,rkhd->rqhd", own_dz, key_four, preferred_element_type=SINGLE)
            + jnp.einsum("rhqs,shd->rqhd", far_dz, key_heads, preferred_element_type=SINGLE)
        ) * scaling
        key_grad = (
            jnp.einsum("rhqk,rqhd->rkhd", own_dz, query_four, preferred_element_type=SINGLE)
            * scaling
        )
        value_grad = jnp.einsum(
            "rhqk,rqhd->rkhd", own_prob.astype(HALF), mixed_grad, preferred_element_type=SINGLE
        )
        key_far_grads.append(
            (
                jnp.einsum("rhqs,rqhd->shd", far_dz, query_four, preferred_element_type=SINGLE)
                * scaling
            ).reshape(total_rows, model_width)
        )
        value_far_grads.append(
            jnp.einsum(
                "rhqs,rqhd->shd", far_prob.astype(HALF), mixed_grad, preferred_element_type=SINGLE
            ).reshape(total_rows, model_width)
        )
        flat_shape = (local_rows, columns, model_width)
        query_low = query_grad.astype(HALF).reshape(flat_shape)
        key_low = key_grad.astype(HALF).reshape(flat_shape)
        value_low = value_grad.astype(HALF).reshape(flat_shape)
        grad_query_w = grad_query_w + outer_dot(attn_in, query_low)
        grad_key_w = grad_key_w + outer_dot(attn_in, key_low)
        grad_value_w = grad_value_w + outer_dot(attn_in, value_low)
        attn_grad = (
            backward_dot(query_low, w_query)
            + backward_dot(key_low, w_key)
            + backward_dot(value_low, w_value)
        )
        grad_gain_one = grad_gain_one + jnp.sum(attn_grad * normed_one, axis=(0, 1))
        partial_inputs.append(
            middle_grad + norm_back(attn_grad * gain_one, normed_one, inverse_one)
        )
    key_far_total, value_far_total = (
        lax.psum_scatter(
            jnp.stack(key_far_grads).astype(jnp.bfloat16), "row", scatter_dimension=1, tiled=True
        ).astype(jnp.float32),
        lax.psum_scatter(
            jnp.stack(value_far_grads).astype(jnp.bfloat16), "row", scatter_dimension=1, tiled=True
        ).astype(jnp.float32),
    )
    key_far_low = key_far_total.astype(HALF)
    value_far_low = value_far_total.astype(HALF)
    grad_key_w = grad_key_w + outer_dot(summary_low, key_far_low)
    grad_value_w = grad_value_w + outer_dot(summary_low, value_far_low)
    summary_grad = backward_dot(key_far_low, w_key) + backward_dot(value_far_low, w_value)
    grad_gain_sum = jnp.sum(summary_grad * standard, axis=(0, 1))
    grad_bias_sum = jnp.sum(summary_grad, axis=(0, 1))
    standard_grad = summary_grad * gain_sum
    plain_total, cross_total = lax.psum(
        (jnp.sum(standard_grad, axis=(0, 1)), jnp.sum(standard_grad * standard, axis=(0, 1))),
        ("img", "row"),
    )
    mean_grad = summary_inv * (
        standard_grad - plain_total / summary_count - standard * (cross_total / summary_count)
    )
    input_grad = jnp.stack(partial_inputs) + mean_grad[:, :, None, :] / columns
    flat_grads = jnp.concatenate(
        [
            grad_gain_one,
            grad_gain_sum,
            grad_bias_sum,
            grad_gain_two,
            grad_query_w.reshape(-1),
            grad_key_w.reshape(-1),
            grad_value_w.reshape(-1),
            grad_out_w.reshape(-1),
            grad_inner_w.reshape(-1),
            grad_outer_w.reshape(-1),
        ]
    )
    weight_grad = lax.psum_scatter(flat_grads, ("img", "row"), scatter_dimension=0, tiled=True)
    return (jnp.stack(outputs), input_grad, weight_grad, summary_mean, summary_var)


def solution(mesh):
    placed = (P("img", "row", None, None), P("img", "row", None, None), P(("img", "row")))
    return jax.shard_map(
        per_device,
        mesh=mesh,
        in_specs=placed,
        out_specs=(
            P("img", "row", None, None),
            P("img", "row", None, None),
            P(("img", "row")),
            P(),
            P(),
        ),
        check_vma=False,
    )
```

profile of v0, /device:TPU:0, one launch (start us, length us, event | category | flops | bytes accessed | tf_op | source)
XLA Modules:
  0.0 783.0 jit_solution(15161708301872468722)
XLA Ops:
  10.4 4.4 dynamic-update-slice
  17.0 43.5 %all-reduce.5 = (f32[512]{0:T(512)S(1)}, f32[512]{0:T(512)S(1)}) all-reduce(f32[512]{0:T(512)S(1)} %get-tuple-element.52, f32[512]{0:T(512)S(1)} %get-tuple-element.51), channel_id=1, replica_groups=mesh['img'=8,'row'=4] {'img','row'}, use_global_device_ids=true, to_apply=%region_5.0 | all-reduce | flops 1024 | bytes 8192 | tf_op jit(solution)/shard_map/psum | solution.py:93
  62.9 112.7 %all-reduce.11.cloned.1.call-done = bf16[3147776]{0:T(1024)(128)(2,1)} async-done(((bf16[3147776]{0:T(1024)(128)(2,1)}), bf16[3147776]{0:T(1024)(128)(2,1)}) %all-reduce.11.cloned.1.call-update) | async-done | bytes 6295568
  197.3 4.5 fusion.290
  201.8 4.3 reshape.416
  207.2 5.4 all_gather.11
  213.7 5.5 all_gather.12
  237.8 4.3 reshape.417
  253.3 4.1 fusion.36
  269.1 4.0 fusion.180
  273.2 6.2 fusion.6
  281.2 6.4 fusion.13
  296.2 4.9 fusion.109
  305.1 4.1 fusion.231
  309.2 4.1 fusion.233
  315.6 5.7 fusion.20
  327.8 4.6 multiply_add_fusion.1
  343.7 5.5 fusion.122
  353.9 5.7 fusion.125
  368.7 5.7 fusion.119
  387.0 15.2 %multiply_reduce_fusion.2 = (f32[4,8,192]{2,1,0:T(8,128)S(1)}, f32[4,8,192]{2,1,0:T(8,128)S(1)}, f32[4,8,192]{2,1,0:T(8,128)S(1)}, f32[4,8,192,192]{2,3,1,0:T(8,128)}) fusion(f32[4,8,192]{2,1,0:T(8,128)} %copy-done.139, f32[4,8,192]{2,1,0:T(8,128)} %copy-done.136, f32[4,8,192,192]{2,3,1,0:T(8,128)} %copy-done.12, ...), kind=kOutput, calls=%fused_computation.47 | convolution fusion | flops 172210176 | bytes 30142464 | tf_op jit(solution)/shard_map/rqhd,rkhd->rhqk/dot_general | solution.py:210
  404.1 15.9 %multiply_convert_fusion.2 = (bf16[4,8,192,192]{2,3,1,0:T(8,128)(2,1)}, bf16[4,8,192,192]{2,3,1,0:T(8,128)(2,1)S(1)}, bf16[4,8,192,192]{2,3,1,0:T(8,128)(2,1)S(1)}) fusion(f32[4,8,192,192]{2,3,1,0:T(8,128)} %get-tuple-element.102, f32[4,8,192]{2,1,0:T(8,128)S(1)} %copy_add_fusion.2, f32[4,8,192]{2,1,0:T(8,128)S(1)} %copy-done.141, ...), kind=kLoop, calls=%fused_computation.46 | loop fusion | flops 24772608 | bytes 35647488 | tf_op jit(solution)/shard_map/convert_element_type | solution.py:219
  420.1 4.2 multiply_convert_fusion.8
  469.4 9.5 %fusion.39 = f32[256,4,8,128]{3,2,1,0:T(8,128)} fusion(f32[2048,512,1]{1,0,2:T(8,128)} %fusion.177, f32[2048,512,1]{1,0,2:T(8,128)S(1)} %copy-done.204, bf16[3,4,192,512]{3,2,1,0:T(8,128)(2,1)} %param.4, f32[4,192,2048]{2,1,0:T(8,128)} %copy-done.54), kind=kOutput, calls=%fused_computation.69 | convolution fusion | flops 1626865664 | bytes 19660800 | tf_op jit(solution)/shard_map/rwd,rwe->de/dot_general | solution.py:58
  479.0 4.2 fusion.40
  494.4 4.1 fusion.96
  508.5 8.9 %all-reduce.15.cloned.1.call-done = (bf16[3,16,512]{2,1,0:T(8,128)(2,1)}, bf16[3,16,512]{2,1,0:T(8,128)(2,1)}) async-done(((bf16[3,16,512]{2,1,0:T(8,128)(2,1)}, bf16[3,16,512]{2,1,0:T(8,128)(2,1)}), (bf16[3,16,512]{2,1,0:T(8,128)(2,1)}, bf16[3,16,512]{2,1,0:T(8,128)(2,1)})) %all-reduce.15.cloned.1.call-update) | async-done | bytes 98320
  541.1 6.1 fusion.142
  547.3 5.1 fusion.143
  563.7 40.9 %all-reduce.4 = (f32[512]{0:T(512)S(1)}, f32[512]{0:T(512)S(1)}) all-reduce(f32[512]{0:T(512)S(1)} %get-tuple-element.40, f32[512]{0:T(512)S(1)} %get-tuple-element.49), channel_id=1, replica_groups=mesh['img'=8,'row'=4] {'img','row'}, use_global_device_ids=true, to_apply=%region_52.53 | all-reduce | flops 1024 | bytes 8192 | tf_op jit(solution)/shard_map/psum | solution.py:275
  604.6 5.3 maximum_add_fusion
  610.0 164.2 %all-reduce.13.cloned.1.call-done = f32[3147776]{0:T(1024)} async-done(((f32[3147776]{0:T(1024)}), f32[3147776]{0:T(1024)}) %all-reduce.13.cloned.1.call-update) | async-done | bytes 12591120
  (632 shorter events, 236.9 us)
Async XLA Ops:
  7.2 168.5 %all-reduce.11.cloned.1.call-start = ((), (), s32[]{:S(2)}) async-start(), calls=%async_computation | async-start | bytes 12591104
  14.7 502.6 %all-reduce.15.cloned.1.call-start = ((), (), s32[]{:S(2)}) async-start(), calls=%async_computation.2 | async-start | bytes 196608
  17.0 174.6 %copy-start.105 = (f32[3,4,512]{2,1,0:T(4,128)}, f32[3,4,512]{2,1,0:T(4,128)S(1)}, u32[]{:S(2)}) copy-start(f32[3,4,512]{2,1,0:T(4,128)S(1)} %convert_reduce_fusion) | copy-start | bytes 73732
  61.1 134.7 %copy-start.160 = (f32[4,192]{1,0:T(4,128)}, f32[4,192]{1,0:T(4,128)S(1)}, u32[]{:S(2)}) copy-start(f32[4,192]{1,0:T(4,128)S(1)} %broadcast_multiply_fusion.17) | copy-start | bytes 9220
  61.1 131.6 %copy-start.168 = (f32[4,192]{1,0:T(4,128)}, f32[4,192]{1,0:T(4,128)S(1)}, u32[]{:S(2)}) copy-start(f32[4,192]{1,0:T(4,128)S(1)} %get-tuple-element.111) | copy-start | bytes 9220
  61.1 133.1 %copy-start.171 = (f32[4,192]{1,0:T(4,128)}, f32[4,192]{1,0:T(4,128)S(1)}, u32[]{:S(2)}) copy-start(f32[4,192]{1,0:T(4,128)S(1)} %get-tuple-element.112) | copy-start | bytes 9220
  62.3 133.5 %copy-start.163 = (f32[4,192]{1,0:T(4,128)}, f32[4,192]{1,0:T(4,128)S(1)}, u32[]{:S(2)}) copy-start(f32[4,192]{1,0:T(4,128)S(1)} %add_rsqrt_fusion.5) | copy-start | bytes 9220
  62.3 130.4 %copy-start.186 = (f32[4,192]{1,0:T(4,128)}, f32[4,192]{1,0:T(4,128)S(1)}, u32[]{:S(2)}) copy-start(f32[4,192]{1,0:T(4,128)S(1)} %add_rsqrt_fusion.1) | copy-start | bytes 9220
  62.3 131.9 %copy-start.189 = (f32[4,192]{1,0:T(4,128)}, f32[4,192]{1,0:T(4,128)S(1)}, u32[]{:S(2)}) copy-start(f32[4,192]{1,0:T(4,128)S(1)} %add_rsqrt_fusion.3) | copy-start | bytes 9220
  62.9 128.7 %copy-start.178 = (f32[512]{0:T(512)}, f32[512]{0:T(512)S(1)}, u32[]{:S(2)}) copy-start(f32[512]{0:T(512)S(1)} %get-tuple-element.61) | copy-start | bytes 6148
  62.9 128.7 %copy-start.180 = (f32[512]{0:T(512)}, f32[512]{0:T(512)S(1)}, u32[]{:S(2)}) copy-start(f32[512]{0:T(512)S(1)} %get-tuple-element.59) | copy-start | bytes 6148
  181.0 14.8 %copy-start.165 = (f32[512]{0:T(512)}, f32[512]{0:T(512)S(1)}, u32[]{:S(2)}) copy-start(f32[512]{0:T(512)S(1)} %get-tuple-element.65) | copy-start | bytes 6148
  207.1 16.4 %copy-start.104 = (bf16[4,192,512]{2,1,0:T(8,128)(2,1)S(1)}, bf16[4,192,512]{2,1,0:T(8,128)(2,1)}, u32[]{:S(2)}) copy-start(bf16[4,192,512]{2,1,0:T(8,128)(2,1)} %convolution_convert_fusion.7) | copy-start | bytes 2359300
  212.8 33.1 %copy-start.120 = (bf16[16,8,64]{2,1,0:T(8,128)(2,1)}, bf16[16,8,64]{2,1,0:T(8,128)(2,1)S(1)}, u32[]{:S(2)}) copy-start(bf16[16,8,64]{2,1,0:T(8,128)(2,1)S(1)} %reshape_squeeze.24) | copy-start | bytes 49156
  212.9 31.8 %copy-start.122 = (bf16[16,8,64]{2,1,0:T(8,128)(2,1)}, bf16[16,8,64]{2,1,0:T(8,128)(2,1)S(1)}, u32[]{:S(2)}) copy-start(bf16[16,8,64]{2,1,0:T(8,128)(2,1)S(1)} %reshape_squeeze.28) | copy-start | bytes 49156
  226.3 19.9 %copy-start.17 = (bf16[4,192,512]{1,2,0:T(8,128)(2,1)}, bf16[4,192,512]{1,2,0:T(8,128)(2,1)S(1)}, u32[]{:S(2)}) copy-start(bf16[4,192,512]{1,2,0:T(8,128)(2,1)S(1)} %copy.379) | copy-start | bytes 2359300
  246.2 17.9 %copy-start.38 = (f32[4,8,192,16]{2,3,0,1:T(8,128)}, f32[4,8,192,16]{2,3,0,1:T(8,128)S(1)}, u32[]{:S(2)}) copy-start(f32[4,8,192,16]{2,3,0,1:T(8,128)S(1)} %get-tuple-element.88) | copy-start | bytes 1179652
  248.1 14.1 %copy-start.12 = (f32[4,8,192,192]{2,3,1,0:T(8,128)}, f32[4,8,192,192]{2,3,1,0:T(8,128)S(1)}, u32[]{:S(2)}) copy-start(f32[4,8,192,192]{2,3,1,0:T(8,128)S(1)} %get-tuple-element.86) | copy-start | bytes 14155780
  248.1 14.1 %copy-start.136 = (f32[4,8,192]{2,1,0:T(8,128)}, f32[4,8,192]{2,1,0:T(8,128)S(1)}, u32[]{:S(2)}) copy-start(f32[4,8,192]{2,1,0:T(8,128)S(1)} %copy_maximum_fusion.2) | copy-start | bytes 73732
  249.1 92.2 %copy-start.42 = (f32[4,8,192,16]{2,3,0,1:T(8,128)}, f32[4,8,192,16]{2,3,0,1:T(8,128)S(1)}, u32[]{:S(2)}) copy-start(f32[4,8,192,16]{2,3,0,1:T(8,128)S(1)} %get-tuple-element.91) | copy-start | bytes 1179652
  261.8 17.6 %copy-start.22 = (f32[4,192,512]{2,1,0:T(8,128)}, f32[4,192,512]{2,1,0:T(8,128)S(1)}, u32[]{:S(2)}) copy-start(f32[4,192,512]{2,1,0:T(8,128)S(1)} %get-tuple-element.97) | copy-start | bytes 4718596
  302.9 24.9 %copy-start.55 = (f32[4,192,512]{2,1,0:T(8,128)}, f32[4,192,512]{2,1,0:T(8,128)S(1)}, u32[]{:S(2)}) copy-start(f32[4,192,512]{2,1,0:T(8,128)S(1)} %get-tuple-element.95) | copy-start | bytes 4718596
  386.9 15.3 %copy-start.176 = (f32[4,8,192]{2,0,1:T(4,128)S(1)}, f32[4,8,192]{2,0,1:T(4,128)}, u32[]{:S(2)}) copy-start(f32[4,8,192]{2,0,1:T(4,128)} %get-tuple-element.107) | copy-start | bytes 73732
  386.9 15.9 %copy-start.177 = (f32[4,8,192]{2,0,1:T(4,128)S(1)}, f32[4,8,192]{2,0,1:T(4,128)}, u32[]{:S(2)}) copy-start(f32[4,8,192]{2,0,1:T(4,128)} %get-tuple-element.105) | copy-start | bytes 73732
  386.9 16.5 %copy-start.175 = (f32[4,8,192]{2,0,1:T(4,128)S(1)}, f32[4,8,192]{2,0,1:T(4,128)}, u32[]{:S(2)}) copy-start(f32[4,8,192]{2,0,1:T(4,128)} %get-tuple-element.103) | copy-start | bytes 73732
  386.9 17.2 %copy-start.117 = (f32[4,8,192]{2,1,0:T(8,128)S(1)}, f32[4,8,192]{2,1,0:T(8,128)}, u32[]{:S(2)}) copy-start(f32[4,8,192]{2,1,0:T(8,128)} %copy-done.115) | copy-start | bytes 73732
  386.9 17.2 %copy-start.138 = (f32[4,8,192]{2,1,0:T(8,128)S(1)}, f32[4,8,192]{2,1,0:T(8,128)}, u32[]{:S(2)}) copy-start(f32[4,8,192]{2,1,0:T(8,128)} %copy-done.136) | copy-start | bytes 73732
  387.0 17.2 %copy-start.141 = (f32[4,8,192]{2,1,0:T(8,128)S(1)}, f32[4,8,192]{2,1,0:T(8,128)}, u32[]{:S(2)}) copy-start(f32[4,8,192]{2,1,0:T(8,128)} %copy-done.139) | copy-start | bytes 73732
  387.0 17.1 %copy-start.144 = (f32[4,8,192]{2,1,0:T(8,128)S(1)}, f32[4,8,192]{2,1,0:T(8,128)}, u32[]{:S(2)}) copy-start(f32[4,8,192]{2,1,0:T(8,128)} %copy-done.142) | copy-start | bytes 73732
  387.0 17.1 %copy-start.147 = (f32[4,8,192]{2,1,0:T(8,128)S(1)}, f32[4,8,192]{2,1,0:T(8,128)}, u32[]{:S(2)}) copy-start(f32[4,8,192]{2,1,0:T(8,128)} %copy-done.145) | copy-start | bytes 73732
  404.1 15.9 %copy-start.18 = (bf16[4,192,512]{1,2,0:T(8,128)(2,1)S(1)}, bf16[4,192,512]{1,2,0:T(8,128)(2,1)}, u32[]{:S(2)}) copy-start(bf16[4,192,512]{1,2,0:T(8,128)(2,1)} %copy-done.17) | copy-start | bytes 2359300
  486.1 288.0 %all-reduce.13.cloned.1.call-start = ((), (), s32[]{:S(2)}) async-start(), calls=%async_computation.1 | async-start | bytes 25182208
  (180 other events, 699.0 us)
Sparse Core Ops, SparseCore 0:
  14.9 160.7 all-reduce.10
  486.2 31.1 all-reduce.14
  541.2 232.9 all-reduce.12
where the time goes:
time: 794 us; the launch traced here: 783 us
  waiting for transfers between devices  286 us (36%)
  matrix products  233 us (29%)
  local copies, waits for them, and re-layouts  108 us (14%)
  blocking collectives  95.1 us (12%)
  other arithmetic  44.1 us (6%)
  between operations  17 us (2%)
    unnamed x6, waiting for transfers between devices  286 us
    dot_general x20, matrix products, backward_dot(): return jnp.einsum('rwe,de->rwd', left, right, preferred_element_type=SINGLE)  56.2 us
    dot_general x20, matrix products, outer_dot(): return jnp.einsum('rwd,rwe->de', left, right, preferred_element_type=SINGLE)  55.4 us
    unnamed x435, local copies, waits for them, and re-layouts  49.7 us
    psum x1, blocking collectives, per_device(): lax.psum((local_first, local_second), ('img', 'row'))  43.5 us
    psum x1, blocking collectives, per_device(): lax.psum((jnp.sum(standard_grad, axis=(0, 1)), jnp.sum(standard_grad * st...  40.9 us
    dot_general x20, matrix products, forward_dot(): return jnp.einsum('rwd,de->rwe', left, right, preferred_element_type=SINGLE)  36.3 us
    dot_general x3, matrix products, per_device(): jnp.einsum('rqhd,rkhd->rhqk', mixed_grad, value_four, preferred_element_t...  22.5 us
  transfers between devices with their start and end apart: 3, of which 3 were waited for; matrix products, arithmetic and copies ran while one was open for 6% of the time, Pallas kernels for 0%

commit v1 on v0

--- a/solution.py
+++ b/solution.py
@@ -15,21 +15,143 @@
 SINGLE = jnp.float32
 
 
-def unpack(flat_weights, model_width, ff_width):
-    lengths = (
-        [model_width] * 4
-        + [model_width * model_width] * 4
-        + [model_width * ff_width, ff_width * model_width]
-    )
-    segments = []
-    offset = 0
-    for length in lengths:
-        segments.append(flat_weights[offset : offset + length])
-        offset = offset + length
-    layouts = [(model_width, model_width)] * 4 + [(model_width, ff_width), (ff_width, model_width)]
-    matrices = [segment.reshape(layout) for segment, layout in zip(segments[4:], layouts)]
-    vectors = [segment.astype(SINGLE) for segment in segments[:4]]
-    return (vectors, matrices)
+TAIL = 16
+
+
+def swap(value, axis, distance):
+    size = lax.axis_size(axis)
+    return lax.ppermute(value, axis, [(i, i ^ distance) for i in range(size)])
+
+
+def hops():
+    rows, images = lax.axis_size("row"), lax.axis_size("img")
+    inner = ("row", 1, 1)
+    across = ("row", 2, 2)
+    along = ("img", 1, rows)
+    outer = []
+    distance = images // 2
+    while distance > 1:
+        outer.append(("img", distance, distance * rows))
+        distance //= 2
+    distance = rows // 2
+    while distance > 2:
+        outer.append(("row", distance, distance))
+        distance //= 2
+    return inner, across, along, outer
+
+
+def piece_order():
+    inner, across, along, outer = hops()
+    masks = [0]
+    for _, _, mask in outer:
+        masks = masks + [m ^ mask for m in masks]
+    near = (
+        masks
+        + [m ^ across[2] for m in masks]
+        + [m ^ along[2] for m in masks]
+        + [m ^ across[2] ^ along[2] for m in masks]
+    )
+    return near + [m ^ inner[2] for m in near]
+
+
+def device_index():
+    return lax.axis_index("img") * lax.axis_size("row") + lax.axis_index("row")
+
+
+def gather_pieces(own):
+    inner, across, along, outer = hops()
+    held = own[None]
+    for axis, distance, _ in outer:
+        held = jnp.concatenate([held, swap(held, axis, distance)])
+    half = held.shape[0] // 2
+    held_x = swap(held, across[0], across[1])
+    held_y = swap(held, along[0], along[1])
+    corner_first = swap(held_x[:half], along[0], along[1])
+    corner_second = swap(held_y[half:], across[0], across[1])
+    near = [held, held_x, held_y, corner_first, corner_second]
+    far = [swap(part, inner[0], inner[1]) for part in near]
+    return jnp.concatenate(near + far)
+
+
+def scatter_pieces(pieces):
+    inner, across, along, outer = hops()
+
+    def add(kept, sent, axis, distance):
+        return kept + swap(sent.astype(HALF), axis, distance).astype(SINGLE)
+
+    count = pieces.shape[0] // 2
+    near = add(pieces[:count], pieces[count:], inner[0], inner[1])
+    quarter = count // 4
+    half = quarter // 2
+    held, held_x, held_y, corner = (near[i * quarter : (i + 1) * quarter] for i in range(4))
+    first = add(
+        jnp.concatenate([held[:half], held_x[:half]]),
+        jnp.concatenate([held_y[:half], corner[:half]]),
+        along[0],
+        along[1],
+    )
+    second = add(
+        jnp.concatenate([held[half:], held_y[half:]]),
+        jnp.concatenate([held_x[half:], corner[half:]]),
+        across[0],
+        across[1],
+    )
+    first = add(first[:half], first[half:], across[0], across[1])
+    second = add(second[:half], second[half:], along[0], along[1])
+    held = jnp.concatenate([first, second])
+    for axis, distance, _ in reversed(outer):
+        half = held.shape[0] // 2
+        held = add(held[:half], held[half:], axis, distance)
+    return held[0]
+
+
+def sum_everywhere(value):
+    inner, across, along, outer = hops()
+    for axis, distance, _ in [inner, across, along] + outer[::-1]:
+        value = value + swap(value, axis, distance)
+    return value
+
+
+def gather_weights(weights, model_width):
+    length = weights.shape[0]
+    me = device_index()
+    devices = lax.axis_size("img") * lax.axis_size("row")
+    block = length // model_width
+    rest = length % model_width
+    start = TAIL * model_width + rest * me - 4 * model_width
+    own = lax.dynamic_update_slice(jnp.zeros(((block + TAIL) * model_width,), HALF), weights, (start,))
+    own = own.reshape(block + TAIL, model_width)
+    pieces = gather_pieces(own)
+    place = [0] * devices
+    for at, mask in enumerate(piece_order()):
+        place[mask] = at
+    order = jnp.asarray(place, jnp.int32)[jnp.arange(devices) ^ me]
+    pieces = jnp.take(pieces, order, axis=0, mode="clip")
+    tails = jnp.concatenate([pieces[1:, :TAIL], jnp.zeros((1, TAIL, model_width), HALF)])
+    body = jnp.concatenate([pieces[:, TAIL:block], pieces[:, block:] + tails], axis=1)
+    return pieces[0, TAIL - 4 : TAIL], body.reshape(devices * block, model_width)
+
+
+def scatter_grads(vectors, rows, length):
+    model_width = rows.shape[1]
+    me = device_index()
+    devices = lax.axis_size("img") * lax.axis_size("row")
+    block = length // model_width
+    rest = length % model_width
+    whole = jnp.concatenate([jnp.zeros((TAIL - 4, model_width), SINGLE), vectors, rows])
+    place = jnp.asarray(piece_order(), jnp.int32)
+    pieces = jnp.stack([whole[block * s : block * s + block + TAIL] for s in range(devices)])
+    pieces = jnp.take(pieces, place ^ me, axis=0, mode="clip")
+    mine = scatter_pieces(pieces)
+    start = TAIL * model_width + rest * me - 4 * model_width
+    return lax.dynamic_slice(mine.reshape(-1), (start,), (length,))
+
+
+def unpack(vectors, rows, model_width, ff_width):
+    matrices = [rows[i * model_width : (i + 1) * model_width] for i in range(4)]
+    matrices.append(rows[4 * model_width : 4 * model_width + ff_width].reshape(model_width, ff_width))
+    matrices.append(rows[4 * model_width + ff_width :])
+    return ([vectors[i].astype(SINGLE) for i in range(4)], matrices)
 
 
 def normalize(values):
@@ -83,14 +205,13 @@
     total_rows = local_rows * lax.axis_size("row")
     first_row = lax.axis_index("row") * local_rows
     summary_count = float(images * lax.axis_size("img") * total_rows)
-    gathered = lax.all_gather(weights, ("img", "row"), axis=0, tiled=True)
-    vectors, matrices = unpack(gathered, model_width, FF)
+    vectors, matrices = unpack(*gather_weights(weights, model_width), model_width, FF)
     gain_one, gain_sum, bias_sum, gain_two = vectors
     w_query, w_key, w_value, w_out, w_inner, w_outer = matrices
     row_means = jnp.mean(activations.astype(SINGLE), axis=2)
     local_first = jnp.sum(row_means, axis=(0, 1))
     local_second = jnp.sum(row_means * row_means, axis=(0, 1))
-    total_first, total_second = lax.psum((local_first, local_second), ("img", "row"))
+    total_first, total_second = sum_everywhere(jnp.stack([local_first, local_second]))
     summary_mean = total_first / summary_count
     summary_var = total_second / summary_count - summary_mean * summary_mean
     summary_inv = lax.rsqrt(summary_var + EPS)
@@ -155,10 +276,6 @@
                 activated,
             )
         )
-    regathered = lax.all_gather(weights, ("img", "row"), axis=0, tiled=True)
-    vectors, matrices = unpack(regathered, model_width, FF)
-    gain_one, gain_sum, bias_sum, gain_two = vectors
-    w_query, w_key, w_value, w_out, w_inner, w_outer = matrices
     grad_gain_one = jnp.zeros((model_width,), SINGLE)
     grad_gain_two = jnp.zeros((model_width,), SINGLE)
     grad_query_w = jnp.zeros((model_width, model_width), SINGLE)
@@ -272,29 +389,25 @@
     grad_gain_sum = jnp.sum(summary_grad * standard, axis=(0, 1))
     grad_bias_sum = jnp.sum(summary_grad, axis=(0, 1))
     standard_grad = summary_grad * gain_sum
-    plain_total, cross_total = lax.psum(
-        (jnp.sum(standard_grad, axis=(0, 1)), jnp.sum(standard_grad * standard, axis=(0, 1))),
-        ("img", "row"),
+    plain_total, cross_total = sum_everywhere(
+        jnp.stack([jnp.sum(standard_grad, axis=(0, 1)), jnp.sum(standard_grad * standard, axis=(0, 1))])
     )
     mean_grad = summary_inv * (
         standard_grad - plain_total / summary_count - standard * (cross_total / summary_count)
     )
     input_grad = jnp.stack(partial_inputs) + mean_grad[:, :, None, :] / columns
-    flat_grads = jnp.concatenate(
+    vectors = jnp.stack([grad_gain_one, grad_gain_sum, grad_bias_sum, grad_gain_two])
+    rows = jnp.concatenate(
         [
-            grad_gain_one,
-            grad_gain_sum,
-            grad_bias_sum,
-            grad_gain_two,
-            grad_query_w.reshape(-1),
-            grad_key_w.reshape(-1),
-            grad_value_w.reshape(-1),
-            grad_out_w.reshape(-1),
-            grad_inner_w.reshape(-1),
-            grad_outer_w.reshape(-1),
+            grad_query_w,
+            grad_key_w,
+            grad_value_w,
+            grad_out_w,
+            grad_inner_w.reshape(-1, model_width),
+            grad_outer_w,
         ]
     )
-    weight_grad = lax.psum_scatter(flat_grads, ("img", "row"), scatter_dimension=0, tiled=True)
+    weight_grad = scatter_grads(vectors, rows, weights.shape[0])
     return (jnp.stack(outputs), input_grad, weight_grad, summary_mean, summary_var)
 
 

time: 794 us -> 618 us (0.78)
  waiting for transfers between devices: 286 us -> 76.6 us
  blocking collectives: 95.1 us -> 10.7 us
  local copies, waits for them, and re-layouts: 108 us -> 149 us
  starting transfers between devices: 0.12 us -> 33.2 us
  matrix products: 233 us -> 257 us
  other arithmetic: 44.1 us -> 60.6 us
    unnamed x6 -> x2, waiting for transfers between devices: 286 us -> 2.58 us
    psum x2 -> x0, blocking collectives: 84.3 us -> none  [the longest x1 43.5 us: per_device(): lax.psum((local_first, local_second), ('img', 'row'))]
    ppermute x0 -> x28, waiting for transfers between devices: none -> 74 us  [swap(): return lax.ppermute(value, axis, [(i, i ^ distance) for i in range(size)])]
    ppermute x0 -> x28, starting transfers between devices: none -> 33.1 us  [swap(): return lax.ppermute(value, axis, [(i, i ^ distance) for i in range(size)])]
    another operation x0 -> x12, local copies, waits for them, and re-layouts: none -> 19.2 us  [the longest x11 19.1 us: scatter_grads(): jnp.stack([whole[block * s:block * s + block + TAIL] for s in range(devic...]
    gather x0 -> x3, local copies, waits for them, and re-layouts: none -> 18.7 us  [the longest x1 11.3 us: scatter_grads(): pieces = jnp.take(pieces, place ^ me, axis=0, mode='clip')]
    unnamed x435 -> x488, local copies, waits for them, and re-layouts: 49.7 us -> 35.2 us
    dot_general x20, matrix products: 56.2 us -> 69.8 us  [backward_dot(): return jnp.einsum('rwe,de->rwd', left, right, preferred_element_type=SINGLE)]
  transfers between devices with their start and end apart: 3 -> 29, of which waited for: 3 -> 15; matrix products, arithmetic and copies ran while one was open for 6% -> 13% of each run, Pallas kernels for 0% -> 0%
where the time goes in v1:
time: 618 us; the launch traced here: 606 us
  matrix products  257 us (42%)
  local copies, waits for them, and re-layouts  149 us (24%)
  waiting for transfers between devices  76.6 us (12%)
  other arithmetic  60.6 us (10%)
  starting transfers between devices  33.2 us (5%)
  between operations  18.1 us (3%)
  blocking collectives  10.7 us (2%)
    ppermute x28, waiting for transfers between devices, swap(): return lax.ppermute(value, axis, [(i, i ^ distance) for i in range(size)])  74 us
    dot_general x20, matrix products, backward_dot(): return jnp.einsum('rwe,de->rwd', left, right, preferred_element_type=SINGLE)  69.8 us
    dot_general x20, matrix products, outer_dot(): return jnp.einsum('rwd,rwe->de', left, right, preferred_element_type=SINGLE)  57.7 us
    dot_general x20, matrix products, forward_dot(): return jnp.einsum('rwd,de->rwe', left, right, preferred_element_type=SINGLE)  42.5 us
    unnamed x488, local copies, waits for them, and re-layouts  35.2 us
    ppermute x28, starting transfers between devices, swap(): return lax.ppermute(value, axis, [(i, i ^ distance) for i in range(size)])  33.1 us
    dot_general x3, matrix products, per_device(): jnp.einsum('rqhd,rkhd->rhqk', mixed_grad, value_four, preferred_element_t...  22.4 us
    another operation x11, local copies, waits for them, and re-layouts, scatter_grads(): jnp.stack([whole[block * s:block * s + block + TAIL] for s in range(devic...  19.1 us
  transfers between devices with their start and end apart: 29, of which 15 were waited for; matrix products, arithmetic and copies ran while one was open for 13% of the time, Pallas kernels for 0%

profile of v1, /device:TPU:0, one launch (start us, length us, event | category | flops | bytes accessed | tf_op | source)
XLA Modules:
  0.0 605.7 jit_solution(17229223218936501646)
XLA Ops:
  19.5 8.6 %collective-permute-done = bf16[1,208,512]{2,1,0:T(8,128)(2,1)S(1)} collective-permute-done((bf16[1,208,512]{2,1,0:T(8,128)(2,1)S(1)}, bf16[1,208,512]{2,1,0:T(8,128)(2,1)S(1)}, u32[]{:S(2)}, u32[]{:S(2)}) %collective-permute-start) | collective-permute-done | bytes 213024 | tf_op jit(solution)/shard_map/ppermute | solution.py:23
  32.1 7.7 %collective-permute-done.1 = bf16[2,208,512]{2,1,0:T(8,128)(2,1)S(1)} collective-permute-done((bf16[2,208,512]{2,1,0:T(8,128)(2,1)S(1)}, bf16[2,208,512]{2,1,0:T(8,128)(2,1)S(1)}, u32[]{:S(2)}, u32[]{:S(2)}) %collective-permute-start.1) | collective-permute-done | bytes 426016 | tf_op jit(solution)/shard_map/ppermute | solution.py:23
  44.3 16.7 %collective-permute-done.13 = f32[2,512]{1,0:T(2,128)S(1)} collective-permute-done((f32[2,512]{1,0:T(2,128)S(1)}, f32[2,512]{1,0:T(2,128)S(1)}, u32[]{:S(2)}, u32[]{:S(2)}) %collective-permute-start.13) | collective-permute-done | bytes 4128 | tf_op jit(solution)/shard_map/ppermute | solution.py:23
  90.1 6.7 %gather_fusion.1 = bf16[32,208,512]{2,1,0:T(8,128)(2,1)} fusion(bf16[32,208,512]{2,1,0:T(8,128)(2,1)} %constant_dynamic-update-slice_fusion.3, s32[1024]{0:T(1024)S(1)} %pad_clamp_fusion.1), kind=kCustom, calls=%fused_computation.1 | custom fusion | bytes 13631616 | tf_op jit(solution)/shard_map/jit(_take)/gather | solution.py:129
  98.8 5.6 slice.360
  105.5 5.9 pad_maximum_fusion
  130.4 5.5 all_gather.7
  136.8 5.2 all_gather.6
  167.8 6.7 %fusion.34 = (f32[4,8,192]{2,1,0:T(8,128)S(1)}, f32[4,8,192]{2,1,0:T(8,128)}, f32[4,8,192]{2,1,0:T(8,128)}, f32[4,8,192,192]{2,3,1,0:T(8,128)}) fusion(f32[4,8,192,192]{2,3,1,0:T(8,128)S(1)} %get-tuple-element.105, f32[4,8,192]{2,1,0:T(8,128)S(1)} %copy_maximum_fusion.2, pred[192,192]{0,1:T(8,128)(4,1)S(1)} %iota_compare_fusion, ...), kind=kOutput, calls=%fused_computation.67 | convolution fusion | flops 162772992 | bytes 15863808 | tf_op jit(solution)/shard_map/rqhd,rkhd->rhqk/dot_general | solution.py:185
  184.3 6.4 %fusion.6 = bf16[4,192,2048]{2,1,0:T(8,128)(2,1)} fusion(f32[4,192,2048]{2,1,0:T(8,128)S(1)} %fusion.256, bf16[3,4,192,512]{3,2,1,0:T(8,128)(2,1)S(1)} %copy-done.151, bf16[6144,512]{1,0:T(8,128)(2,1)S(1)} %bitcast.715), kind=kOutput, calls=%fused_computation.17 | convolution fusion | flops 1642070016 | bytes 12320768 | tf_op jit(solution)/shard_map/rwe,de->rwd/dot_general | solution.py:176
  202.6 7.1 %fusion.36 = (f32[4,8,192]{2,1,0:T(8,128)S(1)}, f32[4,8,192]{2,1,0:T(8,128)S(1)}) fusion(f32[4,8,192,192]{2,3,1,0:T(8,128)} %get-tuple-element.108, f32[4,8,192]{2,1,0:T(8,128)S(1)} %copy_maximum_fusion.1, pred[192,192]{0,1:T(8,128)(4,1)S(1)} %iota_compare_fusion, f32[4,8,192]{2,1,0:T(8,128)S(1)} %copy_maximum_fusion, f32[4,8,192,192]{2,3,1,0:T(8,128)} %copy-done.1), kind=kLoop, calls=%fused_computation.69 | loop fusion | flops 9424896 | bytes 9572352 | tf_op jit(solution)/shard_map/reduce_sum | solution.py:197
  217.6 9.4 %fusion.13 = bf16[4,192,2048]{2,1,0:T(8,128)(2,1)} fusion(f32[4,192,2048]{2,1,0:T(8,128)S(1)} %fusion.258, bf16[3,4,192,512]{3,2,1,0:T(8,128)(2,1)S(1)} %copy-done.152, bf16[6144,512]{1,0:T(8,128)(2,1)} %bitcast.687), kind=kOutput, calls=%fused_computation.24 | convolution fusion | flops 1642070016 | bytes 12320768 | tf_op jit(solution)/shard_map/rwe,de->rwd/dot_general | solution.py:176
  233.7 4.9 fusion.107
  252.0 6.7 %fusion.20 = bf16[4,192,2048]{2,1,0:T(8,128)(2,1)} fusion(f32[4,192,2048]{2,1,0:T(8,128)S(1)} %fusion.259, bf16[3,4,192,512]{3,2,1,0:T(8,128)(2,1)S(1)} %copy-done.153, bf16[6144,512]{1,0:T(8,128)(2,1)S(1)} %bitcast.718), kind=kOutput, calls=%fused_computation.31 | convolution fusion | flops 1642070016 | bytes 12320768 | tf_op jit(solution)/shard_map/rwe,de->rwd/dot_general | solution.py:176
  281.1 5.6 fusion.123
  291.5 5.7 fusion.120
  307.4 5.7 fusion.117
  324.6 15.1 %multiply_reduce_fusion.2 = (f32[4,8,192]{2,1,0:T(8,128)S(1)}, f32[4,8,192]{2,1,0:T(8,128)S(1)}, f32[4,8,192]{2,1,0:T(8,128)S(1)}, f32[4,8,192,192]{2,3,1,0:T(8,128)}) fusion(f32[4,8,192]{2,1,0:T(8,128)S(1)} %copy-done.141, f32[4,8,192]{2,1,0:T(8,128)S(1)} %copy-done.137, f32[4,8,192,192]{2,3,1,0:T(8,128)} %copy-done.15, ...), kind=kOutput, calls=%fused_computation.53 | convolution fusion | flops 172210176 | bytes 30142464 | tf_op jit(solution)/shard_map/rqhd,rkhd->rhqk/dot_general | solution.py:327
  341.6 15.8 %multiply_convert_fusion.2 = (bf16[4,8,192,192]{2,3,1,0:T(8,128)(2,1)}, bf16[4,8,192,192]{2,3,1,0:T(8,128)(2,1)S(1)}, bf16[4,8,192,192]{2,3,1,0:T(8,128)(2,1)S(1)}) fusion(f32[4,8,192,192]{2,3,1,0:T(8,128)} %get-tuple-element.121, f32[4,8,192]{2,1,0:T(8,128)S(1)} %copy_add_fusion.2, f32[4,8,192]{2,1,0:T(8,128)S(1)} %copy-done.142, ...), kind=kLoop, calls=%fused_computation.52 | loop fusion | flops 24772608 | bytes 35647488 | tf_op jit(solution)/shard_map/convert_element_type | solution.py:336
  400.1 5.5 bitcast_add_fusion.2
  421.3 6.2 %fusion.94 = (f32[512]{0:T(512)S(1)}, f32[4,192]{1,0:T(4,128)S(1)}, f32[4,192]{1,0:T(4,128)}, f32[512]{0:T(512)S(1)}, f32[4,192]{1,0:T(4,128)S(1)}, /*index=5*/f...) fusion(f32[4,192]{1,0:T(4,128)S(1)} %copy-done.192, ...), kind=kOutput, calls=%fused_computation.155 | convolution fusion | flops 414050304 | bytes 11579392 | tf_op jit(solution)/shard_map/rwe,de->rwd/dot_general | solution.py:176
  428.8 5.5 bitcast_add_fusion
  441.4 5.4 reshape.446
  475.9 5.3 concatenate.57
  501.2 11.3 %gather_fusion.2 = f32[32,208,512]{2,1,0:T(8,128)} fusion(f32[32,208,512]{2,1,0:T(8,128)} %copy-done.24, s32[1024]{0:T(1024)} %get-tuple-element.132), kind=kCustom, calls=%fused_computation.2 | custom fusion | bytes 27263104 | tf_op jit(solution)/shard_map/jit(_take)/gather | solution.py:144
  512.5 5.4 slice.653
  517.9 6.6 %fusion.137 = bf16[1,4,192,512]{3,2,1,0:T(8,128)(2,1)} fusion(f32[4,192,512]{2,1,0:T(8,128)S(1)} %copy-done.27, bf16[6144,512]{1,0:T(8,128)(2,1)} %bitcast.701, f32[4,192,2048]{2,1,0:T(8,128)} %copy-done.48), kind=kOutput, calls=%fused_computation.248 | convolution fusion | flops 1625554944 | bytes 10747904 | tf_op jit(solution)/shard_map/rwd,de->rwe/dot_general | solution.py:172
  524.7 4.9 fusion.138
  538.5 7.4 %fusion.323 = (bf16[16,208,512]{2,1,0:T(8,128)(2,1)}, f32[16,208,512]{2,1,0:T(8,128)}) fusion(bf16[16,208,512]{2,1,0:T(8,128)(2,1)} %collective-permute-done.21, f32[32,208,512]{2,1,0:T(8,128)S(1)} %bitcast.681), kind=kLoop, calls=%fused_computation.566 | loop fusion | flops 5111808 | bytes 20447232 | tf_op jit(solution)/shard_map/convert.14
  554.9 12.4 %collective-permute-done.24 = bf16[4,208,512]{2,1,0:T(8,128)(2,1)S(1)} collective-permute-done((bf16[4,208,512]{2,1,0:T(8,128)(2,1)S(1)}, bf16[4,208,512]{2,1,0:T(8,128)(2,1)S(1)}, u32[]{:S(2)}, u32[]{:S(2)}) %collective-permute-start.24) | collective-permute-done | bytes 852000 | tf_op jit(solution)/shard_map/ppermute | solution.py:23
  572.7 5.3 collective-permute-done.25
  579.5 8.3 %collective-permute-done.26 = bf16[2,208,512]{2,1,0:T(8,128)(2,1)S(1)} collective-permute-done((bf16[2,208,512]{2,1,0:T(8,128)(2,1)S(1)}, bf16[2,208,512]{2,1,0:T(8,128)(2,1)S(1)}, u32[]{:S(2)}, u32[]{:S(2)}) %collective-permute-start.26) | collective-permute-done | bytes 426016 | tf_op jit(solution)/shard_map/ppermute | solution.py:23
  (796 shorter events, 347.1 us)
Async XLA Ops:
  7.2 461.3 %all-reduce.6.cloned.1.call-start = ((), (), s32[]{:S(2)}) async-start(), calls=%async_computation | async-start | bytes 196608
  9.5 20.3 %collective-permute-start.11 = (f32[2,512]{1,0:T(2,128)S(1)}, f32[2,512]{1,0:T(2,128)S(1)}, u32[]{:S(2)}, u32[]{:S(2)}) collective-permute-start(f32[2,512]{1,0:T(2,128)S(1)} %pad_maximum_fusion.12), channel_id=1, source_target_pairs={{0,1},{1,0},{2,3},{3,2},{4,5},{5,4},{6,7},{7,6},{8,9},{9,8},{10,11... | collective-permute-start | bytes 12296 | tf_op jit(solution)/shard_map/ppermute | solution.py:23
  14.0 14.1 %collective-permute-start = (bf16[1,208,512]{2,1,0:T(8,128)(2,1)S(1)}, bf16[1,208,512]{2,1,0:T(8,128)(2,1)S(1)}, u32[]{:S(2)}, u32[]{:S(2)}) collective-permute-start(bf16[1,208,512]{2,1,0:T(8,128)(2,1)S(1)} %broadcast_in_dim_reshape.3), channel_id=1, source_target_pairs={{0,16},{4,20},{8,24},{12,28},{16,0},{20,4},{24,8},{28,12},{1,17},{... | collective-permute-start | bytes 638984 | tf_op jit(solution)/shard_map/ppermute | solution.py:23
  18.2 109.2 %copy-start.163 = (f32[4,192]{1,0:T(4,128)}, f32[4,192]{1,0:T(4,128)S(1)}, u32[]{:S(2)}) copy-start(f32[4,192]{1,0:T(4,128)S(1)} %broadcast_multiply_fusion.17) | copy-start | bytes 9220
  18.2 105.5 %copy-start.174 = (f32[4,192]{1,0:T(4,128)}, f32[4,192]{1,0:T(4,128)S(1)}, u32[]{:S(2)}) copy-start(f32[4,192]{1,0:T(4,128)S(1)} %get-tuple-element.130) | copy-start | bytes 9220
  19.4 108.0 %copy-start.168 = (f32[4,192]{1,0:T(4,128)}, f32[4,192]{1,0:T(4,128)S(1)}, u32[]{:S(2)}) copy-start(f32[4,192]{1,0:T(4,128)S(1)} %add_rsqrt_fusion.5) | copy-start | bytes 9220
  28.1 11.7 %collective-permute-start.1 = (bf16[2,208,512]{2,1,0:T(8,128)(2,1)S(1)}, bf16[2,208,512]{2,1,0:T(8,128)(2,1)S(1)}, u32[]{:S(2)}, u32[]{:S(2)}) collective-permute-start(bf16[2,208,512]{2,1,0:T(8,128)(2,1)S(1)} %pad_maximum_fusion.9), channel_id=1, source_target_pairs={{0,8},{4,12},{8,0},{12,4},{16,24},{20,28},{24,16},{28,20},{1,9},{5... | collective-permute-start | bytes 1277960 | tf_op jit(solution)/shard_map/ppermute | solution.py:23
  29.7 14.0 %collective-permute-start.12 = (f32[2,512]{1,0:T(2,128)S(1)}, f32[2,512]{1,0:T(2,128)S(1)}, u32[]{:S(2)}, u32[]{:S(2)}) collective-permute-start(f32[2,512]{1,0:T(2,128)S(1)} %fusion.289), channel_id=1, source_target_pairs={{0,2},{1,3},{2,0},{3,1},{4,6},{5,7},{6,4},{7,5},{8,10},{9,11},{10,... | collective-permute-start | bytes 12296 | tf_op jit(solution)/shard_map/ppermute | solution.py:23
  40.8 28.5 %collective-permute-start.3 = (bf16[4,208,512]{2,1,0:T(8,128)(2,1)}, bf16[4,208,512]{2,1,0:T(8,128)(2,1)S(1)}, u32[]{:S(2)}, u32[]{:S(2)}) collective-permute-start(bf16[4,208,512]{2,1,0:T(8,128)(2,1)} %get-tuple-element.85), channel_id=1, source_target_pairs={{0,4},{4,0},{8,12},{12,8},{16,20},{20,16},{24,28},{28,24},{1,5},{5... | collective-permute-start | bytes 2555912 | tf_op jit(solution)/shard_map/ppermute | solution.py:23
  42.2 28.7 %collective-permute-start.2 = (bf16[4,208,512]{2,1,0:T(8,128)(2,1)}, bf16[4,208,512]{2,1,0:T(8,128)(2,1)}, u32[]{:S(2)}, u32[]{:S(2)}) collective-permute-start(bf16[4,208,512]{2,1,0:T(8,128)(2,1)} %get-tuple-element.85), channel_id=1, source_target_pairs={{0,2},{1,3},{2,0},{3,1},{4,6},{5,7},{6,4},{7,5},{8,10},{9,11},{10,... | collective-permute-start | bytes 2555912 | tf_op jit(solution)/shard_map/ppermute | solution.py:23
  43.8 17.3 %collective-permute-start.13 = (f32[2,512]{1,0:T(2,128)S(1)}, f32[2,512]{1,0:T(2,128)S(1)}, u32[]{:S(2)}, u32[]{:S(2)}) collective-permute-start(f32[2,512]{1,0:T(2,128)S(1)} %fusion.417), channel_id=1, source_target_pairs={{0,4},{4,0},{8,12},{12,8},{16,20},{20,16},{24,28},{28,24},{1,5},{5... | collective-permute-start | bytes 12296 | tf_op jit(solution)/shard_map/ppermute | solution.py:23
  61.0 3.6 collective-permute-start.14
  64.6 4.6 collective-permute-start.15
  69.3 16.3 %collective-permute-start.6 = (bf16[4,208,512]{2,1,0:T(8,128)(2,1)}, bf16[4,208,512]{2,1,0:T(8,128)(2,1)S(1)}, u32[]{:S(2)}, u32[]{:S(2)}) collective-permute-start(bf16[4,208,512]{2,1,0:T(8,128)(2,1)} %get-tuple-element.85), channel_id=1, source_target_pairs={{0,1},{1,0},{2,3},{3,2},{4,5},{5,4},{6,7},{7,6},{8,9},{9,8},{10,11... | collective-permute-start | bytes 2555912 | tf_op jit(solution)/shard_map/ppermute | solution.py:23
  69.4 12.3 %collective-permute-start.5 = (bf16[2,208,512]{2,1,0:T(8,128)(2,1)S(1)}, bf16[2,208,512]{2,1,0:T(8,128)(2,1)S(1)}, u32[]{:S(2)}, u32[]{:S(2)}) collective-permute-start(bf16[2,208,512]{2,1,0:T(8,128)(2,1)S(1)} %slice.358), channel_id=1, source_target_pairs={{0,2},{1,3},{2,0},{3,1},{4,6},{5,7},{6,4},{7,5},{8,10},{9,11},{10,... | collective-permute-start | bytes 1277960 | tf_op jit(solution)/shard_map/ppermute | solution.py:23
  72.0 12.0 %collective-permute-start.4 = (bf16[2,208,512]{2,1,0:T(8,128)(2,1)S(1)}, bf16[2,208,512]{2,1,0:T(8,128)(2,1)S(1)}, u32[]{:S(2)}, u32[]{:S(2)}) collective-permute-start(bf16[2,208,512]{2,1,0:T(8,128)(2,1)S(1)} %slice.357), channel_id=1, source_target_pairs={{0,4},{4,0},{8,12},{12,8},{16,20},{20,16},{24,28},{28,24},{1,5},{5... | collective-permute-start | bytes 1277960 | tf_op jit(solution)/shard_map/ppermute | solution.py:23
  73.5 14.0 %collective-permute-start.8 = (bf16[4,208,512]{2,1,0:T(8,128)(2,1)S(1)}, bf16[4,208,512]{2,1,0:T(8,128)(2,1)S(1)}, u32[]{:S(2)}, u32[]{:S(2)}) collective-permute-start(bf16[4,208,512]{2,1,0:T(8,128)(2,1)S(1)} %collective-permute-done.3), channel_id=1, source_target_pairs={{0,1},{1,0},{2,3},{3,2},{4,5},{5,4},{6,7},{7,6},{8,9},{9,8},{10,11... | collective-permute-start | bytes 2555912 | tf_op jit(solution)/shard_map/ppermute | solution.py:23
  73.5 13.0 %collective-permute-start.7 = (bf16[4,208,512]{2,1,0:T(8,128)(2,1)}, bf16[4,208,512]{2,1,0:T(8,128)(2,1)S(1)}, u32[]{:S(2)}, u32[]{:S(2)}) collective-permute-start(bf16[4,208,512]{2,1,0:T(8,128)(2,1)} %collective-permute-done.2), channel_id=1, source_target_pairs={{0,1},{1,0},{2,3},{3,2},{4,5},{5,4},{6,7},{7,6},{8,9},{9,8},{10,11... | collective-permute-start | bytes 2555912 | tf_op jit(solution)/shard_map/ppermute | solution.py:23
  81.6 7.7 %collective-permute-start.10 = (bf16[2,208,512]{2,1,0:T(8,128)(2,1)S(1)}, bf16[2,208,512]{2,1,0:T(8,128)(2,1)S(1)}, u32[]{:S(2)}, u32[]{:S(2)}) collective-permute-start(bf16[2,208,512]{2,1,0:T(8,128)(2,1)S(1)} %collective-permute-done.5), channel_id=1, source_target_pairs={{0,1},{1,0},{2,3},{3,2},{4,5},{5,4},{6,7},{7,6},{8,9},{9,8},{10,11... | collective-permute-start | bytes 1277960 | tf_op jit(solution)/shard_map/ppermute | solution.py:23
  84.0 4.6 collective-permute-start.9
  517.9 20.6 %collective-permute-start.21 = (bf16[16,208,512]{2,1,0:T(8,128)(2,1)}, bf16[16,208,512]{2,1,0:T(8,128)(2,1)}, u32[]{:S(2)}, u32[]{:S(2)}) collective-permute-start(bf16[16,208,512]{2,1,0:T(8,128)(2,1)} %slice.653), channel_id=1, source_target_pairs={{0,1},{1,0},{2,3},{3,2},{4,5},{5,4},{6,7},{7,6},{8,9},{9,8},{10,11... | collective-permute-start | bytes 10223624 | tf_op jit(solution)/shard_map/ppermute | solution.py:23
  529.6 3.7 collective-permute-start.16
  533.3 3.7 collective-permute-start.17
  537.0 11.4 %collective-permute-start.18 = (f32[2,512]{1,0:T(2,128)S(1)}, f32[2,512]{1,0:T(2,128)S(1)}, u32[]{:S(2)}, u32[]{:S(2)}) collective-permute-start(f32[2,512]{1,0:T(2,128)S(1)} %fusion.416), channel_id=1, source_target_pairs={{0,4},{4,0},{8,12},{12,8},{16,20},{20,16},{24,28},{28,24},{1,5},{5... | collective-permute-start | bytes 12296 | tf_op jit(solution)/shard_map/ppermute | solution.py:23
  547.7 19.5 %collective-permute-start.24 = (bf16[4,208,512]{2,1,0:T(8,128)(2,1)S(1)}, bf16[4,208,512]{2,1,0:T(8,128)(2,1)S(1)}, u32[]{:S(2)}, u32[]{:S(2)}) collective-permute-start(bf16[4,208,512]{2,1,0:T(8,128)(2,1)S(1)} %pad_maximum_fusion.3), channel_id=1, source_target_pairs={{0,2},{1,3},{2,0},{3,1},{4,6},{5,7},{6,4},{7,5},{8,10},{9,11},{10,... | collective-permute-start | bytes 2555912 | tf_op jit(solution)/shard_map/ppermute | solution.py:23
  548.4 3.7 collective-permute-start.19
  550.0 19.9 %collective-permute-start.22 = (bf16[4,208,512]{2,1,0:T(8,128)(2,1)S(1)}, bf16[4,208,512]{2,1,0:T(8,128)(2,1)S(1)}, u32[]{:S(2)}, u32[]{:S(2)}) collective-permute-start(bf16[4,208,512]{2,1,0:T(8,128)(2,1)S(1)} %pad_maximum_fusion.2), channel_id=1, source_target_pairs={{0,4},{4,0},{8,12},{12,8},{16,20},{20,16},{24,28},{28,24},{1,5},{5... | collective-permute-start | bytes 2555912 | tf_op jit(solution)/shard_map/ppermute | solution.py:23
  552.1 17.9 %collective-permute-start.20 = (f32[2,512]{1,0:T(2,128)S(1)}, f32[2,512]{1,0:T(2,128)S(1)}, u32[]{:S(2)}, u32[]{:S(2)}) collective-permute-start(f32[2,512]{1,0:T(2,128)S(1)} %add.481), channel_id=1, source_target_pairs={{0,16},{4,20},{8,24},{12,28},{16,0},{20,4},{24,8},{28,12},{1,17},{... | collective-permute-start | bytes 12296 | tf_op jit(solution)/shard_map/ppermute | solution.py:23
  567.6 10.5 %collective-permute-start.25 = (bf16[2,208,512]{2,1,0:T(8,128)(2,1)S(1)}, bf16[2,208,512]{2,1,0:T(8,128)(2,1)S(1)}, u32[]{:S(2)}, u32[]{:S(2)}) collective-permute-start(bf16[2,208,512]{2,1,0:T(8,128)(2,1)S(1)} %slice.654), channel_id=1, source_target_pairs={{0,4},{4,0},{8,12},{12,8},{16,20},{20,16},{24,28},{28,24},{1,5},{5... | collective-permute-start | bytes 1277960 | tf_op jit(solution)/shard_map/ppermute | solution.py:23
  570.3 9.2 %collective-permute-start.23 = (bf16[2,208,512]{2,1,0:T(8,128)(2,1)S(1)}, bf16[2,208,512]{2,1,0:T(8,128)(2,1)S(1)}, u32[]{:S(2)}, u32[]{:S(2)}) collective-permute-start(bf16[2,208,512]{2,1,0:T(8,128)(2,1)S(1)} %slice.655), channel_id=1, source_target_pairs={{0,2},{1,3},{2,0},{3,1},{4,6},{5,7},{6,4},{7,5},{8,10},{9,11},{10,... | collective-permute-start | bytes 1277960 | tf_op jit(solution)/shard_map/ppermute | solution.py:23
  578.2 9.5 %collective-permute-start.26 = (bf16[2,208,512]{2,1,0:T(8,128)(2,1)S(1)}, bf16[2,208,512]{2,1,0:T(8,128)(2,1)S(1)}, u32[]{:S(2)}, u32[]{:S(2)}) collective-permute-start(bf16[2,208,512]{2,1,0:T(8,128)(2,1)S(1)} %fusion.166), channel_id=1, source_target_pairs={{0,8},{4,12},{8,0},{12,4},{16,24},{20,28},{24,16},{28,20},{1,9},{5... | collective-permute-start | bytes 1277960 | tf_op jit(solution)/shard_map/ppermute | solution.py:23
  588.0 9.3 %collective-permute-start.27 = (bf16[1,208,512]{2,1,0:T(8,128)(2,1)S(1)}, bf16[1,208,512]{2,1,0:T(8,128)(2,1)S(1)}, u32[]{:S(2)}, u32[]{:S(2)}) collective-permute-start(bf16[1,208,512]{2,1,0:T(8,128)(2,1)S(1)} %slice.656), channel_id=1, source_target_pairs={{0,16},{4,20},{8,24},{12,28},{16,0},{20,4},{24,8},{28,12},{1,17},{... | collective-permute-start | bytes 638984 | tf_op jit(solution)/shard_map/ppermute | solution.py:23
  (222 other events, 1902.4 us)
Sparse Core Ops, SparseCore 0:
  436.5 31.9 all-reduce.5
